TPU v7x, 32 devices: a whole 2x2x4 slice. The times are simulated.
32 devices in a mesh: dp: 16 (over z, y, core), mod: 2 (over x).
Axes of the slice: x: 2, y: 2, z: 4, core: 2. Of those that a mesh axis runs over, the one named last changes fastest.
Arguments:
- tokens: bfloat16 [8192, 1152], P(('dp', 'mod')), may hold values from -6 to 6
- condition: bfloat16 [256, 1152], P('dp'), may hold values from -6 to 6
- lengths: int32 [64, 4], P(('dp', 'mod')), may hold values from 1 to 64, 128 in all within a row
- positions: int32 [2, 8192], P(None, ('dp', 'mod')), may hold values from 0 to 31
- query_gain: float32 [72], replicated, may hold values from 0.25 to 1.75
- key_gain: float32 [72], replicated, may hold values from 0.25 to 1.75
- attend_in: bfloat16 [1152, 3456], P('dp', 'mod'), may hold values from -0.1875 to 0.1875
- attend_out: bfloat16 [1152, 1152], P('dp', 'mod'), may hold values from -0.375 to 0.375
- feed_in: bfloat16 [1152, 6144], P('dp', 'mod'), may hold values from -0.1875 to 0.1875
- feed_out: bfloat16 [3072, 1152], P('dp', 'mod'), may hold values from -0.15625 to 0.15625
- modulate_weight: bfloat16 [1152, 6912], P('dp', 'mod'), may hold values from -0.25 to 0.25
- cotangent: bfloat16 [8192, 1152], P(('dp', 'mod')), may hold values from -6 to 6
Outputs:
- block_out: bfloat16 [8192, 1152], P(('dp', 'mod'))
- tokens_grad: float32 [8192, 1152], P(('dp', 'mod'))
- condition_grad: float32 [256, 1152], P('dp', 'mod')
- query_gain_grad: float32 [72], replicated
- key_gain_grad: float32 [72], replicated
- attend_in_grad: float32 [1152, 3456], P('dp', 'mod')
- attend_out_grad: float32 [1152, 1152], P('dp', 'mod')
- feed_in_grad: float32 [1152, 6144], P('dp', 'mod')
- feed_out_grad: float32 [3072, 1152], P('dp', 'mod')
- modulate_grad: float32 [1152, 6912], P('dp', 'mod')
Inputs may be any that keep to these rules, and one draw needn't show every extreme that they name: `lengths`: row j lists in order the token counts of the 4 images packed into sequence j, whose conditioning vectors are condition rows j * 4 to j * 4 + 3; each row sums to 128 and holds one image of exactly 64 tokens.
All inputs are finite; a program needn't handle non-finite values.
Results may differ from a plain program's by a relative error of at most 0.018.
Values may be sent and summed in bfloat16 or wider, within the bound.
No kernel may reach another device: no remote copies, remote signals or barrier semaphores. Data moves between devices by JAX's collectives and lax.ppermute only.
A program may use at most 256 MiB of HBM per device.

v0:
```python
import jax
import jax.numpy as jnp
from jax import lax
from jax.sharding import PartitionSpec as P

HIGHEST = lax.Precision.HIGHEST


def item_index(lengths_row, count):
    ends = jnp.cumsum(lengths_row, dtype=jnp.int32)
    places = jnp.arange(count, dtype=jnp.int32)
    return jnp.sum((places[:, None] >= ends[None, :]).astype(jnp.int32), axis=1, dtype=jnp.int32)


def rope_tables(places, head):
    quarter = head // 4
    index = jnp.arange(head, dtype=jnp.int32)
    freq = jnp.power(10000.0, -(index % quarter).astype(jnp.float32) / quarter)
    which = index // (head // 2)
    spot = jnp.where(which[None, :] == 0, places[0][:, None], places[1][:, None]).astype(
        jnp.float32
    )
    angle = spot * freq[None, :]
    return (jnp.cos(angle), jnp.sin(angle))


def rotate(values):
    shape = values.shape
    halves = values.reshape(shape[:-1] + (2, 2, shape[-1] // 4))
    turned = jnp.concatenate([-halves[..., 1:2, :], halves[..., 0:1, :]], axis=-2)
    return turned.reshape(shape)


def layer_norm(values):
    average = jnp.mean(values, axis=-1, keepdims=True)
    centred = values - average
    spread = jnp.mean(centred * centred, axis=-1, keepdims=True)
    inverse = lax.rsqrt(spread + 1e-06)
    return (centred * inverse, inverse)


def norm_back(upstream, normed, inverse):
    first = jnp.mean(upstream, axis=-1, keepdims=True)
    second = jnp.mean(upstream * normed, axis=-1, keepdims=True)
    return inverse * (upstream - first - normed * second)


def rms_forward(values, gain):
    inverse = lax.rsqrt(jnp.mean(values * values, axis=-1, keepdims=True) + 1e-06)
    return (values * inverse * gain, inverse)


def rms_back(upstream, values, inverse, gain):
    scaled = upstream * gain
    inner = jnp.mean(scaled * values, axis=-1, keepdims=True)
    return inverse * scaled - values * inverse * inverse * inverse * inner


def contract_rows(left, right):
    return lax.dot_general(
        left, right, (((0,), (0,)), ((), ())), preferred_element_type=jnp.float32
    )


def contract_cols(left, right):
    return lax.dot_general(
        left, right, (((1,), (1,)), ((), ())), preferred_element_type=jnp.float32
    )


def micro_step(tokens, mods, lengths_row, places, query_gain, key_gain, weights, cotangent):
    attend_in, attend_out, feed_in, feed_out = weights
    count, width = tokens.shape
    head = query_gain.shape[0]
    heads = width // head
    scale = head ** (-0.5)
    items = item_index(lengths_row, count)
    members = items[:, None] == jnp.arange(lengths_row.shape[0], dtype=jnp.int32)[None, :]
    onehot = members.astype(jnp.float32)
    token_mod = jnp.dot(members.astype(jnp.bfloat16), mods, preferred_element_type=jnp.float32)
    shift_attend, scale_attend, gate_attend, shift_feed, scale_feed, gate_feed = jnp.split(
        token_mod, 6, axis=1
    )
    inputs = tokens.astype(jnp.float32)
    normed_one, inverse_one = layer_norm(inputs)
    modded_one = (normed_one * (1.0 + scale_attend) + shift_attend).astype(jnp.bfloat16)
    projected = jnp.dot(modded_one, attend_in, preferred_element_type=jnp.float32).reshape(
        count, 3, heads, head
    )
    query_raw = projected[:, 0]
    key_raw = projected[:, 1]
    values_low = projected[:, 2].astype(jnp.bfloat16)
    query_norm, query_inverse = rms_forward(query_raw, query_gain)
    key_norm, key_inverse = rms_forward(key_raw, key_gain)
    cosine, sine = rope_tables(places, head)
    cosine = cosine[:, None, :]
    sine = sine[:, None, :]
    query_rot = (query_norm * cosine + rotate(query_norm) * sine).astype(jnp.bfloat16)
    key_rot = (key_norm * cosine + rotate(key_norm) * sine).astype(jnp.bfloat16)
    same_item = (items[:, None] == items[None, :])[None]

    def scores_of():
        raw = (
            jnp.einsum("shd,thd->hst", query_rot, key_rot, preferred_element_type=jnp.float32)
            * scale
        )
        return jnp.where(same_item, raw, -1e30)

    scores = scores_of()
    peak = jnp.max(scores, axis=-1, keepdims=True)
    exponent = jnp.exp(scores - peak)
    total = jnp.sum(exponent, axis=-1, keepdims=True)
    log_total = peak + jnp.log(total)
    prob_low = (exponent / total).astype(jnp.bfloat16)
    mixed = jnp.einsum("hst,thd->shd", prob_low, values_low, preferred_element_type=jnp.float32)
    mixed = mixed.reshape(count, width).astype(jnp.bfloat16)
    attended = jnp.dot(mixed, attend_out, preferred_element_type=jnp.float32)
    resid = inputs + gate_attend * attended
    normed_two, inverse_two = layer_norm(resid)
    modded_two = (normed_two * (1.0 + scale_feed) + shift_feed).astype(jnp.bfloat16)
    gate_up = jnp.dot(modded_two, feed_in, preferred_element_type=jnp.float32)
    gate_part, up_part = jnp.split(gate_up, 2, axis=1)
    silu_gate = jax.nn.silu(gate_part)
    hidden = (silu_gate * up_part).astype(jnp.bfloat16)
    fed = jnp.dot(hidden, feed_out, preferred_element_type=jnp.float32)
    output = (resid + gate_feed * fed).astype(jnp.bfloat16)
    upstream = cotangent.astype(jnp.float32)
    fed_grad = (gate_feed * upstream).astype(jnp.bfloat16)
    hidden_grad = contract_cols(fed_grad, feed_out)
    sigma = jax.nn.sigmoid(gate_part)
    silu_slope = sigma * (1.0 + gate_part * (1.0 - sigma))
    gate_up_grad = jnp.concatenate(
        [hidden_grad * up_part * silu_slope, hidden_grad * silu_gate], axis=1
    ).astype(jnp.bfloat16)
    modded_two_grad = contract_cols(gate_up_grad, feed_in)
    resid_grad = upstream + norm_back(modded_two_grad * (1.0 + scale_feed), normed_two, inverse_two)
    attended_grad = (gate_attend * resid_grad).astype(jnp.bfloat16)
    mixed_grad = contract_cols(attended_grad, attend_out).astype(jnp.bfloat16)
    mixed_grad = mixed_grad.reshape(count, heads, head)
    probs = jnp.exp(scores_of() - log_total)
    prob_grad = jnp.einsum(
        "shd,thd->hst", mixed_grad, values_low, preferred_element_type=jnp.float32
    )
    inner = jnp.sum(probs * prob_grad, axis=-1, keepdims=True)
    score_grad = (probs * (prob_grad - inner)).astype(jnp.bfloat16)
    query_rot_grad = (
        jnp.einsum("hst,thd->shd", score_grad, key_rot, preferred_element_type=jnp.float32) * scale
    )
    key_rot_grad = (
        jnp.einsum("hst,shd->thd", score_grad, query_rot, preferred_element_type=jnp.float32)
        * scale
    )
    values_grad = jnp.einsum(
        "hst,shd->thd", probs.astype(jnp.bfloat16), mixed_grad, preferred_element_type=jnp.float32
    )
    query_norm_grad = query_rot_grad * cosine - rotate(query_rot_grad * sine)
    key_norm_grad = key_rot_grad * cosine - rotate(key_rot_grad * sine)
    query_gain_grad = jnp.sum(query_norm_grad * query_raw * query_inverse, axis=(0, 1))
    key_gain_grad = jnp.sum(key_norm_grad * key_raw * key_inverse, axis=(0, 1))
    query_grad = rms_back(query_norm_grad, query_raw, query_inverse, query_gain)
    key_grad = rms_back(key_norm_grad, key_raw, key_inverse, key_gain)
    projected_grad = (
        jnp.stack([query_grad, key_grad, values_grad], axis=1)
        .reshape(count, 3 * width)
        .astype(jnp.bfloat16)
    )
    modded_one_grad = contract_cols(projected_grad, attend_in)
    tokens_grad = resid_grad + norm_back(
        modded_one_grad * (1.0 + scale_attend), normed_one, inverse_one
    )
    token_mod_grad = jnp.concatenate(
        [
            modded_one_grad,
            modded_one_grad * normed_one,
            resid_grad * attended,
            modded_two_grad,
            modded_two_grad * normed_two,
            upstream * fed,
        ],
        axis=1,
    )
    mods_grad = lax.dot_general(onehot, token_mod_grad, (((0,), (0,)), ((), ())), precision=HIGHEST)
    return (
        output,
        tokens_grad,
        mods_grad,
        (modded_one, mixed, modded_two, hidden),
        (projected_grad, attended_grad, gate_up_grad, fed_grad),
        (query_gain_grad, key_gain_grad),
    )


def body(
    tokens,
    condition,
    lengths,
    positions,
    query_gain,
    key_gain,
    attend_in,
    attend_out,
    feed_in,
    feed_out,
    modulate_weight,
    cotangent,
):
    micro = lengths.shape[0]
    count = tokens.shape[0] // micro
    width = tokens.shape[1]
    items_seq = lengths.shape[1]
    hidden_units = feed_out.shape[0] * lax.axis_size("dp")
    modulate_full = lax.all_gather(modulate_weight, "dp", axis=0, tiled=True)
    cond_float = condition.astype(jnp.float32)
    silu_cond = jax.nn.silu(cond_float).astype(jnp.bfloat16)
    mod_columns = jnp.dot(silu_cond, modulate_full, preferred_element_type=jnp.float32).astype(
        jnp.bfloat16
    )
    own_mods = lax.all_to_all(mod_columns, "mod", split_axis=0, concat_axis=1, tiled=True)
    weight_sums = (
        jnp.zeros((width, attend_in.shape[1]), jnp.float32),
        jnp.zeros((width, attend_out.shape[1]), jnp.float32),
        jnp.zeros((width, feed_in.shape[1]), jnp.float32),
        jnp.zeros((hidden_units, feed_out.shape[1]), jnp.float32),
    )
    outputs = []
    token_grads = []
    item_grads = []
    for step in range(micro):
        current = (
            lax.all_gather(
                lax.all_gather(attend_in, "mod", axis=1, tiled=True), "dp", axis=0, tiled=True
            ),
            lax.all_gather(
                lax.all_gather(attend_out, "mod", axis=1, tiled=True), "dp", axis=0, tiled=True
            ),
            lax.all_gather(
                lax.all_gather(feed_in, "mod", axis=1, tiled=True), "dp", axis=0, tiled=True
            ),
            lax.all_gather(
                lax.all_gather(feed_out, "mod", axis=1, tiled=True), "dp", axis=0, tiled=True
            ),
        )
        result = micro_step(
            tokens[step * count : (step + 1) * count],
            own_mods[step * items_seq : (step + 1) * items_seq],
            lengths[step],
            positions[:, step * count : (step + 1) * count],
            query_gain,
            key_gain,
            current,
            cotangent[step * count : (step + 1) * count],
        )
        outputs.append(result[0])
        token_grads.append(result[1])
        item_grads.append(result[2])
        kept = result[3]
        grads_out = result[4]
        group_grads = (
            lax.all_to_all(grads_out[0], "mod", split_axis=1, concat_axis=0, tiled=True),
            lax.all_to_all(grads_out[1], "mod", split_axis=1, concat_axis=0, tiled=True),
            lax.all_to_all(grads_out[2], "mod", split_axis=1, concat_axis=0, tiled=True),
            lax.all_to_all(grads_out[3], "mod", split_axis=1, concat_axis=0, tiled=True),
        )
        pieces = (
            lax.all_gather(kept[0], "mod", axis=0, tiled=True),
            lax.all_gather(kept[1], "mod", axis=0, tiled=True),
            lax.all_gather(kept[2], "mod", axis=0, tiled=True),
            lax.all_gather(kept[3], "mod", axis=0, tiled=True),
        )
        weight_sums = tuple(
            (
                weight_sums[index] + contract_rows(pieces[index], group_grads[index])
                for index in range(4)
            )
        )
        gain_sums = result[5] if step == 0 else jax.tree.map(jnp.add, gain_sums, result[5])
    block_out = jnp.concatenate(outputs, axis=0)
    tokens_grad = jnp.concatenate(token_grads, axis=0)
    own_mod_grad = jnp.concatenate(item_grads, axis=0).astype(jnp.bfloat16)
    mod_column_grad = lax.all_to_all(own_mod_grad, "mod", split_axis=1, concat_axis=0, tiled=True)
    modulate_local = contract_rows(silu_cond, mod_column_grad)
    cond_terms = contract_cols(mod_column_grad, modulate_full)
    cond_share = lax.psum_scatter(
        cond_terms.astype(jnp.bfloat16), "mod", scatter_dimension=1, tiled=True
    ).astype(jnp.float32)
    share = cond_share.shape[1]
    cond_cols = lax.dynamic_slice_in_dim(cond_float, lax.axis_index("mod") * share, share, 1)
    sigma = jax.nn.sigmoid(cond_cols)
    condition_grad = cond_share * sigma * (1.0 + cond_cols * (1.0 - sigma))
    shards = (
        lax.psum_scatter(
            weight_sums[0].astype(jnp.bfloat16), "dp", scatter_dimension=0, tiled=True
        ).astype(jnp.float32),
        lax.psum_scatter(
            weight_sums[1].astype(jnp.bfloat16), "dp", scatter_dimension=0, tiled=True
        ).astype(jnp.float32),
        lax.psum_scatter(
            weight_sums[2].astype(jnp.bfloat16), "dp", scatter_dimension=0, tiled=True
        ).astype(jnp.float32),
        lax.psum_scatter(
            weight_sums[3].astype(jnp.bfloat16), "dp", scatter_dimension=0, tiled=True
        ).astype(jnp.float32),
        lax.psum_scatter(
            modulate_local.astype(jnp.bfloat16), "dp", scatter_dimension=0, tiled=True
        ).astype(jnp.float32),
    )
    gain_totals = lax.psum((gain_sums[0], gain_sums[1]), ("dp", "mod"))
    return (
        block_out,
        tokens_grad,
        condition_grad,
        gain_totals[0],
        gain_totals[1],
        shards[0],
        shards[1],
        shards[2],
        shards[3],
        shards[4],
    )


def solution(mesh):
    placed = (
        P(("dp", "mod"), None),
        P("dp", None),
        P(("dp", "mod"), None),
        P(None, ("dp", "mod")),
        P(),
        P(),
        P("dp", "mod"),
        P("dp", "mod"),
        P("dp", "mod"),
        P("dp", "mod"),
        P("dp", "mod"),
        P(("dp", "mod"), None),
    )
    return jax.shard_map(
        body,
        mesh=mesh,
        in_specs=placed,
        out_specs=(
            P(("dp", "mod"), None),
            P(("dp", "mod"), None),
            P("dp", "mod"),
            P(),
            P(),
            P("dp", "mod"),
            P("dp", "mod"),
            P("dp", "mod"),
            P("dp", "mod"),
            P("dp", "mod"),
        ),
        check_vma=False,
    )
```

profile of v0, /device:TPU:0, one launch (start us, length us, event | category | flops | bytes accessed | tf_op | source)
XLA Modules:
  0.0 960.9 jit_solution(2322314757637098953)
XLA Ops:
  8.0 10.1 %all-gather = bf16[2,1728,72]{1,2,0:T(8,128)(2,1)S(1)} all-gather(bf16[1,1728,72]{1,2,0:T(8,128)(2,1)} %bitcast.362), channel_id=1, replica_groups=mesh['dp'=16,'mod'=2] {'mod'}, dimensions={0}, use_global_device_ids=true | all-gather | bytes 746496 | tf_op jit(solution)/shard_map/all_gather | solution.py:231
  26.2 11.0 %all_gather.64 = bf16[72,6144]{1,0:T(8,128)(2,1)} all-gather(bf16[72,3072]{1,0:T(8,128)(2,1)S(1)} %copy-done.70), channel_id=1, replica_groups=mesh['dp'=16,'mod'=2] {'mod'}, dimensions={1}, use_global_device_ids=true | all-gather | bytes 1327104 | tf_op jit(solution)/shard_map/all_gather | solution.py:237
  49.2 36.0 %all-gather.11.cloned.1.call-done = bf16[1152,3456]{1,0:T(8,128)(2,1)} async-done(((bf16[72,3456]{1,0:T(8,128)(2,1)}), bf16[1152,3456]{1,0:T(8,128)(2,1)}) %all-gather.11.cloned.1.call-update) | async-done | bytes 7962640 | tf_op jit(solution)/shard_map/all_gather | solution.py:212
  101.4 57.0 %all-gather.13.cloned.1.call-done = bf16[1152,3456]{1,0:T(8,128)(2,1)} async-done(((bf16[72,3456]{1,0:T(8,128)(2,1)}), bf16[1152,3456]{1,0:T(8,128)(2,1)}) %all-gather.13.cloned.1.call-update) | async-done | bytes 7962640 | tf_op jit(solution)/shard_map/all_gather | solution.py:230
  170.7 32.2 %all-gather.15.cloned.1.call-done = bf16[1152,1152]{1,0:T(8,128)(2,1)} async-done(((bf16[72,1152]{1,0:T(8,128)(2,1)}), bf16[1152,1152]{1,0:T(8,128)(2,1)}) %all-gather.15.cloned.1.call-update) | async-done | bytes 2654224 | tf_op jit(solution)/shard_map/all_gather | solution.py:233
  206.5 10.3 %all_gather.71 = bf16[256,1152]{0,1:T(8,128)(2,1)} all-gather(bf16[128,1152]{0,1:T(8,128)(2,1)S(1)} %bitcast.359), channel_id=1, replica_groups=mesh['dp'=16,'mod'=2] {'mod'}, dimensions={0}, use_global_device_ids=true | all-gather | bytes 884736 | tf_op jit(solution)/shard_map/all_gather | solution.py:266
  220.8 93.5 %all-gather.17.cloned.1.call-done = bf16[1152,6144]{1,0:T(8,128)(2,1)} async-done(((bf16[72,6144]{1,0:T(8,128)(2,1)}), bf16[1152,6144]{1,0:T(8,128)(2,1)}) %all-gather.17.cloned.1.call-update) | async-done | bytes 14155792 | tf_op jit(solution)/shard_map/all_gather | solution.py:236
  314.3 9.0 fusion.137
  323.3 58.5 %all-gather.19.cloned.1.call-done = bf16[3072,1152]{1,0:T(8,128)(2,1)} async-done(((bf16[192,1152]{1,0:T(8,128)(2,1)}), bf16[3072,1152]{1,0:T(8,128)(2,1)}) %all-gather.19.cloned.1.call-update) | async-done | bytes 7077904 | tf_op jit(solution)/shard_map/all_gather | solution.py:239
  381.9 7.4 multiply_convert_fusion.1
  389.3 11.1 %fusion.123 = (f32[128]{0:T(128)S(1)}, f32[128]{0:T(128)S(1)}, f32[128,1152]{1,0:T(8,128)}) fusion(f32[128,6912]{1,0:T(8,128)S(1)} %fusion.106, f32[128]{0:T(128)S(1)} %copy-done.107, f32[128,1152]{1,0:T(8,128)S(1)} %copy-done.12, f32[128]{0:T(128)S(1)} %copy-done.102, bf16[1152,6144]{1,0:T(8,128)(2,1)} %all-gather.17.cloned.1.call-done, ...), kind=kOutput, calls=%fused_computation.306 | convolution fusion | flops 1816116992 | bytes 17500160 | tf_op jit(solution)/shard_map/dot_general | solution.py:66
  440.8 11.1 %fusion.125 = (f32[128]{0:T(128)S(1)}, f32[128]{0:T(128)S(1)}, f32[128,1152]{1,0:T(8,128)}) fusion(f32[128,6912]{1,0:T(8,128)S(1)} %copy-done.10, f32[128]{0:T(128)S(1)} %add_rsqrt_fusion.6, f32[128,1152]{1,0:T(8,128)S(1)} %get-tuple-element.44, f32[128]{0:T(128)S(1)} %broadcast_multiply_fusion.22, bf16[1152,6144]{1,0:T(8,128)(2,1)} %all-gather.17.cloned.1.call-done, ...), kind=kOutput, calls=%fused_computation.308 | convolution fusion | flops 1816116992 | bytes 17500160 | tf_op jit(solution)/shard_map/dot_general | solution.py:66
  498.5 15.3 %all_gather.70 = bf16[256,1152]{0,1:T(8,128)(2,1)} all-gather(bf16[128,1152]{0,1:T(8,128)(2,1)S(1)} %bitcast.357), channel_id=1, replica_groups=mesh['dp'=16,'mod'=2] {'mod'}, dimensions={0}, use_global_device_ids=true | all-gather | bytes 884736 | tf_op jit(solution)/shard_map/all_gather | solution.py:266
  541.4 12.2 %all_to_all.172 = bf16[128,2,1728]{0,2,1:T(8,128)(2,1)S(1)} all-to-all(bf16[128,2,1728]{0,2,1:T(8,128)(2,1)} %bitcast.322), channel_id=1, replica_groups=mesh['dp'=16,'mod'=2] {'mod'}, dimensions={1} | all-to-all | bytes 1769472 | tf_op jit(solution)/shard_map/all_to_all | solution.py:259
  557.3 15.8 %all_gather.69 = bf16[256,1152]{1,0:T(8,128)(2,1)} all-gather(bf16[128,1152]{1,0:T(8,128)(2,1)S(1)} %copy-done.37), channel_id=1, replica_groups=mesh['dp'=16,'mod'=2] {'mod'}, dimensions={0}, use_global_device_ids=true | all-gather | bytes 884736 | tf_op jit(solution)/shard_map/all_gather | solution.py:265
  573.1 7.7 all_gather.68
  622.6 14.9 %all-to-all-done.6 = bf16[128,2,3072]{2,0,1:T(8,128)(2,1)S(1)} async-done(((bf16[128,2,3072]{2,0,1:T(8,128)(2,1)}), bf16[128,2,3072]{2,0,1:T(8,128)(2,1)S(1)}, u32[]{:S(2)}, u32[]{:S(2)}) %all-to-all-start.6) | async-done | bytes 1572896 | tf_op jit(solution)/shard_map/all_to_all | solution.py:261
  641.3 18.6 %all_gather.73 = bf16[256,1152]{1,0:T(8,128)(2,1)} all-gather(bf16[128,1152]{1,0:T(8,128)(2,1)S(1)} %copy-done.35), channel_id=1, replica_groups=mesh['dp'=16,'mod'=2] {'mod'}, dimensions={0}, use_global_device_ids=true | all-gather | bytes 884736 | tf_op jit(solution)/shard_map/all_gather | solution.py:267
  659.9 7.6 all_gather.72
  674.6 10.3 %fusion = bf16[1152,3072]{1,0:T(8,128)(2,1)} fusion(f32[1152,3072]{1,0:T(8,128)} %fusion.139, bf16[256,1152]{1,0:T(8,128)(2,1)} %all_gather.73, bf16[256,3072]{1,0:T(8,128)(2,1)S(1)} %bitcast.323), kind=kOutput, calls=%fused_computation.2 | convolution fusion | flops 1819017216 | bytes 23396352 | tf_op jit(solution)/shard_map/dot_general | solution.py:60
  691.9 38.8 %all-reduce.2 = (f32[72]{0:T(128)}, f32[72]{0:T(128)}) all-reduce(f32[72]{0:T(128)S(1)} %add.264, f32[72]{0:T(128)S(1)} %add.265), channel_id=1, replica_groups=mesh['dp'=16,'mod'=2] {'dp','mod'}, use_global_device_ids=true, to_apply=%region_37.38 | all-reduce | flops 144 | bytes 1152 | tf_op jit(solution)/shard_map/psum | solution.py:307
  737.8 16.1 %reduce-scatter.17.cloned.1.call-done = bf16[192,576]{1,0:T(8,128)(2,1)} async-done(((bf16[3072,576]{1,0:T(8,128)(2,1)}), bf16[192,576]{1,0:T(8,128)(2,1)}) %reduce-scatter.17.cloned.1.call-update) | async-done | bytes 221200 | tf_op jit(solution)/shard_map/reduce_scatter | solution.py:300
  755.7 91.7 %reduce-scatter.15.cloned.1.call-done = bf16[72,3072]{1,0:T(8,128)(2,1)} async-done(((bf16[1152,3072]{1,0:T(8,128)(2,1)}), bf16[72,3072]{1,0:T(8,128)(2,1)}) %reduce-scatter.15.cloned.1.call-update) | async-done | bytes 442384 | tf_op jit(solution)/shard_map/reduce_scatter | solution.py:297
  849.4 102.4 %reduce-scatter.23.cloned.1.call-done = bf16[72,3456]{1,0:T(8,128)(2,1)} async-done(((bf16[1152,3456]{1,0:T(8,128)(2,1)}), bf16[72,3456]{1,0:T(8,128)(2,1)}) %reduce-scatter.23.cloned.1.call-update) | async-done | bytes 497680
  (509 shorter events, 246.0 us)
Async XLA Ops:
  7.2 77.9 %all-gather.11.cloned.1.call-start = ((), (), s32[]{:S(2)}) async-start(), calls=%async_computation.16 | async-start | bytes 8460288 | tf_op jit(solution)/shard_map/all_gather | solution.py:212
  7.9 150.5 %all-gather.13.cloned.1.call-start = ((), (), s32[]{:S(2)}) async-start(), calls=%async_computation.17 | async-start | bytes 8460288 | tf_op jit(solution)/shard_map/all_gather | solution.py:230
  19.7 183.2 %all-gather.15.cloned.1.call-start = ((), (), s32[]{:S(2)}) async-start(), calls=%async_computation.18 | async-start | bytes 2820096 | tf_op jit(solution)/shard_map/all_gather | solution.py:233
  25.2 59.9 %copy-start.68 = (bf16[16,1152]{1,0:T(8,128)(2,1)S(1)}, bf16[16,1152]{1,0:T(8,128)(2,1)}, u32[]{:S(2)}) copy-start(bf16[16,1152]{1,0:T(8,128)(2,1)} %param.13) | copy-start | bytes 110596
  26.1 288.2 %all-gather.17.cloned.1.call-start = ((), (), s32[]{:S(2)}) async-start(), calls=%async_computation.19 | async-start | bytes 15040512 | tf_op jit(solution)/shard_map/all_gather | solution.py:236
  37.2 344.7 %all-gather.19.cloned.1.call-start = ((), (), s32[]{:S(2)}) async-start(), calls=%async_computation.20 | async-start | bytes 7520256 | tf_op jit(solution)/shard_map/all_gather | solution.py:239
  90.2 7.7 all-to-all-start
  93.6 508.0 %all-gather.21.cloned.1.call-start = ((), (), s32[]{:S(2)}) async-start(), calls=%async_computation.23 | async-start | bytes 2359296 | tf_op jit(solution)/shard_map/all_gather | solution.py:268
  99.2 290.0 %copy-start.9 = (f32[128,6912]{1,0:T(8,128)}, f32[128,6912]{1,0:T(8,128)S(1)}, u32[]{:S(2)}) copy-start(f32[128,6912]{1,0:T(8,128)S(1)} %fusion.106) | copy-start | bytes 10616836
  467.3 140.3 %all-gather.23.cloned.1.call-start = ((), (), s32[]{:S(2)}) async-start(), calls=%async_computation.24 | async-start | bytes 2359296 | tf_op jit(solution)/shard_map/all_gather | solution.py:268
  495.1 20.5 %all-to-all-start.1 = ((bf16[8,2,3456]{2,0,1:T(8,128)(2,1)}), bf16[8,2,3456]{2,0,1:T(8,128)(2,1)S(1)}, u32[]{:S(2)}, u32[]{:S(2)}) async-start(bf16[8,2,3456]{2,0,1:T(8,128)(2,1)} %pad_maximum_fusion.12), calls=%async_computation.1 | async-start | bytes 221184 | tf_op jit(solution)/shard_map/all_to_all | solution.py:280
  515.6 12.7 %all-to-all-start.4 = ((bf16[128,2,576]{0,2,1:T(8,128)(2,1)}), bf16[128,2,576]{0,2,1:T(8,128)(2,1)S(1)}, u32[]{:S(2)}, u32[]{:S(2)}) async-start(bf16[128,2,576]{0,2,1:T(8,128)(2,1)} %bitcast.76), calls=%async_computation.5 | async-start | bytes 589824 | tf_op jit(solution)/shard_map/all_to_all | solution.py:260
  519.2 213.5 %reduce-scatter.19.cloned.1.call-start = ((), (), s32[]{:S(2)}) async-start(), calls=%async_computation.26 | async-start | bytes 442368
  528.3 10.2 %all-to-all-start.5 = ((bf16[128,2,576]{0,2,1:T(8,128)(2,1)}), bf16[128,2,576]{0,2,1:T(8,128)(2,1)}, u32[]{:S(2)}, u32[]{:S(2)}) async-start(bf16[128,2,576]{0,2,1:T(8,128)(2,1)} %bitcast.79), calls=%async_computation.6 | async-start | bytes 589824 | tf_op jit(solution)/shard_map/all_to_all | solution.py:260
  532.5 202.0 %reduce-scatter.21.cloned.1.call-start = ((), (), s32[]{:S(2)}) async-start(), calls=%async_computation.27 | async-start | bytes 1566720
  553.6 27.7 %all-to-all-start.3 = ((bf16[128,2,1728]{0,2,1:T(8,128)(2,1)}), bf16[128,2,1728]{0,2,1:T(8,128)(2,1)S(1)}, u32[]{:S(2)}, u32[]{:S(2)}) async-start(bf16[128,2,1728]{0,2,1:T(8,128)(2,1)} %bitcast.320), calls=%async_computation.3 | async-start | bytes 1769472 | tf_op jit(solution)/shard_map/all_to_all | solution.py:259
  557.2 178.9 %reduce-scatter.13.cloned.1.call-start = ((), (), s32[]{:S(2)}) async-start(), calls=%async_computation.21 | async-start | bytes 4386816 | tf_op jit(solution)/shard_map/reduce_scatter | solution.py:291
  588.4 9.6 all-to-all-start.8
  598.0 9.6 %all-to-all-start.9 = ((bf16[128,2,576]{0,2,1:T(8,128)(2,1)}), bf16[128,2,576]{0,2,1:T(8,128)(2,1)S(1)}, u32[]{:S(2)}, u32[]{:S(2)}) async-start(bf16[128,2,576]{0,2,1:T(8,128)(2,1)} %bitcast.91), calls=%async_computation.11 | async-start | bytes 589824 | tf_op jit(solution)/shard_map/all_to_all | solution.py:262
  601.4 152.5 %reduce-scatter.17.cloned.1.call-start = ((), (), s32[]{:S(2)}) async-start(), calls=%async_computation.25 | async-start | bytes 4177920 | tf_op jit(solution)/shard_map/reduce_scatter | solution.py:300
  617.6 20.0 %all-to-all-start.6 = ((bf16[128,2,3072]{2,0,1:T(8,128)(2,1)}), bf16[128,2,3072]{2,0,1:T(8,128)(2,1)S(1)}, u32[]{:S(2)}, u32[]{:S(2)}) async-start(bf16[128,2,3072]{2,0,1:T(8,128)(2,1)} %pad_maximum_fusion), calls=%async_computation.7 | async-start | bytes 3145728 | tf_op jit(solution)/shard_map/all_to_all | solution.py:261
  637.6 37.0 %all-to-all-start.7 = ((bf16[128,2,3072]{2,0,1:T(8,128)(2,1)}), bf16[128,2,3072]{2,0,1:T(8,128)(2,1)S(1)}, u32[]{:S(2)}, u32[]{:S(2)}) async-start(bf16[128,2,3072]{2,0,1:T(8,128)(2,1)} %pad_maximum_fusion.1), calls=%async_computation.8 | async-start | bytes 3145728 | tf_op jit(solution)/shard_map/all_to_all | solution.py:261
  641.2 206.1 %reduce-scatter.15.cloned.1.call-start = ((), (), s32[]{:S(2)}) async-start(), calls=%async_computation.22 | async-start | bytes 7520256 | tf_op jit(solution)/shard_map/reduce_scatter | solution.py:297
  684.8 267.0 %reduce-scatter.23.cloned.1.call-start = ((), (), s32[]{:S(2)}) async-start(), calls=%async_computation.28 | async-start | bytes 8460288
  (142 other events, 1122.4 us)
Sparse Core Ops, SparseCore 0:
  10.2 74.8 all-gather.10
  87.9 70.5 all-gather.12
  161.2 41.6 all-gather.14
  205.0 109.2 all-gather.16
  317.1 64.7 all-gather.18
  467.4 25.6 all-gather.20
  494.7 34.5 all-gather.22
  531.5 10.3 reduce-scatter.18
  545.7 60.1 reduce-scatter.20
  609.6 70.8 reduce-scatter.12
  684.4 69.4 reduce-scatter.16
  758.3 89.0 reduce-scatter.14
  851.4 100.3 reduce-scatter.22
where the time goes:
time: 971 us; the launch traced here: 961 us
  waiting for transfers between devices  518 us (53%)
  matrix products  162 us (17%)
  blocking collectives  160 us (16%)
  other arithmetic  38.8 us (4%)
  starting transfers between devices  33.3 us (3%)
  local copies, waits for them, and re-layouts  32.5 us (3%)
  between operations  16.2 us (2%)
    unnamed x16, waiting for transfers between devices  103 us
    all_gather x1, waiting for transfers between devices, body(): lax.all_gather(lax.all_gather(feed_in, 'mod', axis=1, tiled=True), 'dp',...  93.5 us
    reduce_scatter x1, waiting for transfers between devices, body(): lax.psum_scatter(weight_sums[2].astype(jnp.bfloat16), 'dp', scatter_dimen...  91.7 us
    all_gather x1, waiting for transfers between devices, body(): lax.all_gather(lax.all_gather(feed_out, 'mod', axis=1, tiled=True), 'dp',...  58.5 us
    all_gather x1, waiting for transfers between devices, body(): lax.all_gather(lax.all_gather(attend_in, 'mod', axis=1, tiled=True), 'dp'...  57 us
    dot_general x9, matrix products, contract_cols(): lax.dot_general(left, right, (((1,), (1,)), ((), ())), preferred_element_...  51.5 us
    dot_general x9, matrix products, contract_rows(): lax.dot_general(left, right, (((0,), (0,)), ((), ())), preferred_element_...  45.3 us
    psum x1, blocking collectives, body(): gain_totals = lax.psum((gain_sums[0], gain_sums[1]), ('dp', 'mod'))  38.8 us
  transfers between devices with their start and end apart: 22, of which 13 were waited for; matrix products, arithmetic and copies ran while one was open for 14% of the time, Pallas kernels for 0%

commit v1 on v0

v1 whole, which is shorter than its diff:
```python
import functools

import jax
import jax.numpy as jnp
from jax import lax
from jax.experimental import pallas as pl
from jax.experimental.pallas import tpu as pltpu
from jax.sharding import PartitionSpec as P

HIGHEST = lax.Precision.HIGHEST
BF = jnp.bfloat16
F32 = jnp.float32
VMEM_LIMIT = 48 * 1024 * 1024


def layer_norm(values):
    average = jnp.mean(values, axis=-1, keepdims=True)
    centred = values - average
    spread = jnp.mean(centred * centred, axis=-1, keepdims=True)
    inverse = lax.rsqrt(spread + 1e-06)
    return (centred * inverse, inverse)


def norm_back(upstream, normed, inverse):
    first = jnp.mean(upstream, axis=-1, keepdims=True)
    second = jnp.mean(upstream * normed, axis=-1, keepdims=True)
    return inverse * (upstream - first - normed * second)


def dot(left, right, left_dim=1, right_dim=0):
    return lax.dot_general(
        left, right, (((left_dim,), (right_dim,)), ((), ())), preferred_element_type=F32
    )


def turned(values, first):
    quarter = values.shape[0] // 4
    ahead = pltpu.roll(values, values.shape[0] - quarter, 0)
    behind = pltpu.roll(values, quarter, 0)
    return jnp.where(first, ahead, behind)


def rms(values):
    return lax.rsqrt(jnp.mean(values * values, axis=0, keepdims=True) + 1e-06)


def scores_t(key_rot, query_rot, same, scale):
    raw = dot(key_rot, query_rot, 0, 0) * scale
    return jnp.where(same, raw, -1e30)


def softmax_t(scores):
    peak = jnp.max(scores, axis=0, keepdims=True)
    exponent = jnp.exp(scores - peak)
    return exponent / jnp.sum(exponent, axis=0, keepdims=True)


def first_mask(head, count):
    row = lax.broadcasted_iota(jnp.int32, (head, count), 0)
    return lax.rem(row, head // 2) < head // 4


def attend_forward_kernel(
    heads, head, modded_ref, weight_ref, cos_ref, sin_ref, qg_ref, kg_ref, row_ref, col_ref,
    raw_ref, low_ref, mixed_ref,
):
    count = modded_ref.shape[0]
    own = heads * head
    projected = jnp.dot(modded_ref[...], weight_ref[...], preferred_element_type=F32).T
    raw_ref[0] = projected[: 2 * own]
    values = projected[2 * own :].astype(BF)
    low_ref[0] = values
    same = col_ref[0] == row_ref[0]
    first = first_mask(head, count)
    cosine, sine = cos_ref[0], sin_ref[0]
    scale = head ** (-0.5)

    def rotated(raw, gain):
        normed = raw * rms(raw) * gain
        return (normed * cosine + turned(normed, first) * sine).astype(BF)

    for h in range(heads):
        query_rot = rotated(projected[h * head : (h + 1) * head], qg_ref[...])
        key_rot = rotated(projected[own + h * head : own + (h + 1) * head], kg_ref[...])
        prob = softmax_t(scores_t(key_rot, query_rot, same, scale)).astype(BF)
        mixed = dot(values[h * head : (h + 1) * head], prob)
        mixed_ref[h * head : (h + 1) * head, :] = mixed.astype(BF)


def attend_backward_kernel(
    heads, head, grad_ref, weight_ref, raw_ref, low_ref, cos_ref, sin_ref, qg_ref, kg_ref, row_ref,
    col_ref, out_ref, qgg_ref, kgg_ref, held_ref,
):
    count = grad_ref.shape[0]
    own = heads * head
    mixed_grad = dot(weight_ref[...], grad_ref[...], 1, 1).astype(BF)
    same = col_ref[0] == row_ref[0]
    first = first_mask(head, count)
    cosine, sine = cos_ref[0], sin_ref[0]
    scale = head ** (-0.5)

    @pl.when(pl.program_id(0) == 0)
    def _():
        qgg_ref[...] = jnp.zeros_like(qgg_ref)
        kgg_ref[...] = jnp.zeros_like(kgg_ref)

    def rotated(raw, gain):
        inverse = rms(raw)
        normed = raw * inverse * gain
        return inverse, (normed * cosine + turned(normed, first) * sine).astype(BF)

    def back(rot_grad, raw, inverse, gain):
        norm_grad = rot_grad * cosine + turned(rot_grad * sine, first)
        gain_grad = norm_grad * raw * inverse
        scaled = norm_grad * gain
        inner = jnp.mean(scaled * raw, axis=0, keepdims=True)
        return inverse * scaled - raw * (inverse * inverse * inverse * inner), gain_grad

    query_total = jnp.zeros((head, count), F32)
    key_total = jnp.zeros((head, count), F32)
    for h in range(heads):
        rows = slice(h * head, (h + 1) * head)
        query_raw = raw_ref[0, h * head : (h + 1) * head]
        key_raw = raw_ref[0, own + h * head : own + (h + 1) * head]
        values = low_ref[0, h * head : (h + 1) * head]
        upstream = mixed_grad[rows]
        query_inverse, query_rot = rotated(query_raw, qg_ref[...])
        key_inverse, key_rot = rotated(key_raw, kg_ref[...])
        prob = softmax_t(scores_t(key_rot, query_rot, same, scale))
        prob_grad = dot(values, upstream, 0, 0)
        inner = jnp.sum(prob * prob_grad, axis=0, keepdims=True)
        score_grad = (prob * (prob_grad - inner)).astype(BF)
        query_rot_grad = dot(key_rot, score_grad) * scale
        key_rot_grad = dot(query_rot, score_grad, 1, 1) * scale
        values_grad = dot(upstream, prob.astype(BF), 1, 1)
        query_grad, query_part = back(query_rot_grad, query_raw, query_inverse, qg_ref[...])
        key_grad, key_part = back(key_rot_grad, key_raw, key_inverse, kg_ref[...])
        query_total += query_part
        key_total += key_part
        held_ref[h * head : (h + 1) * head, :] = query_grad
        held_ref[own + h * head : own + (h + 1) * head, :] = key_grad
        held_ref[2 * own + h * head : 2 * own + (h + 1) * head, :] = values_grad
    qgg_ref[...] += query_total
    kgg_ref[...] += key_total
    out_ref[...] = held_ref[...].T.astype(BF)


def whole_spec(shape):
    return pl.BlockSpec(shape, lambda i: (0,) * len(shape))


def lead_spec(shape):
    return pl.BlockSpec((1,) + shape[1:], lambda i: (i,) + (0,) * (len(shape) - 1))


def attend_forward(modded, weight, cosine, sine, qg, kg, row, col, heads):
    seqs, head, count = cosine.shape
    width = modded.shape[1]
    own = heads * head
    flops = 2 * seqs * count * (width * 3 * own + 2 * count * own)
    return pl.pallas_call(
        functools.partial(attend_forward_kernel, heads, head),
        grid=(seqs,),
        in_specs=[
            pl.BlockSpec((count, width), lambda i: (i, 0)),
            whole_spec(weight.shape),
            lead_spec(cosine.shape),
            lead_spec(sine.shape),
            whole_spec(qg.shape),
            whole_spec(kg.shape),
            lead_spec(row.shape),
            lead_spec(col.shape),
        ],
        out_specs=[
            lead_spec((seqs, 2 * own, count)),
            lead_spec((seqs, own, count)),
            pl.BlockSpec((own, count), lambda i: (0, i)),
        ],
        out_shape=[
            jax.ShapeDtypeStruct((seqs, 2 * own, count), F32),
            jax.ShapeDtypeStruct((seqs, own, count), BF),
            jax.ShapeDtypeStruct((own, seqs * count), BF),
        ],
        compiler_params=pltpu.CompilerParams(vmem_limit_bytes=VMEM_LIMIT),
        cost_estimate=pl.CostEstimate(
            flops=flops, bytes_accessed=10 * 2**20, transcendentals=seqs * heads * count * count
        ),
        name="attend_forward",
    )(modded, weight, cosine, sine, qg, kg, row, col)


def attend_backward(grad, weight, raw, low, cosine, sine, qg, kg, row, col, heads):
    seqs, head, count = cosine.shape
    width = grad.shape[1]
    own = heads * head
    flops = 2 * seqs * count * (width * own + 5 * count * own)
    return pl.pallas_call(
        functools.partial(attend_backward_kernel, heads, head),
        grid=(seqs,),
        in_specs=[
            pl.BlockSpec((count, width), lambda i: (i, 0)),
            whole_spec(weight.shape),
            lead_spec(raw.shape),
            lead_spec(low.shape),
            lead_spec(cosine.shape),
            lead_spec(sine.shape),
            whole_spec(qg.shape),
            whole_spec(kg.shape),
            lead_spec(row.shape),
            lead_spec(col.shape),
        ],
        out_specs=[
            pl.BlockSpec((count, 3 * own), lambda i: (i, 0)),
            whole_spec((head, count)),
            whole_spec((head, count)),
        ],
        out_shape=[
            jax.ShapeDtypeStruct((seqs * count, 3 * own), BF),
            jax.ShapeDtypeStruct((head, count), F32),
            jax.ShapeDtypeStruct((head, count), F32),
        ],
        scratch_shapes=[pltpu.VMEM((3 * own, count), F32)],
        compiler_params=pltpu.CompilerParams(vmem_limit_bytes=VMEM_LIMIT),
        cost_estimate=pl.CostEstimate(
            flops=flops, bytes_accessed=10 * 2**20, transcendentals=seqs * heads * count * count
        ),
        name="attend_backward",
    )(grad, weight, raw, low, cosine, sine, qg, kg, row, col)


def body(
    tokens,
    condition,
    lengths,
    positions,
    query_gain,
    key_gain,
    attend_in,
    attend_out,
    feed_in,
    feed_out,
    modulate_weight,
    cotangent,
):
    ndp, nmod = lax.axis_size("dp"), lax.axis_size("mod")
    planes = ndp // 2
    dp, mod = lax.axis_index("dp"), lax.axis_index("mod")
    core, plane, side = dp % 2, dp // 2, mod % 2
    own_seqs, items_seq = lengths.shape
    own_count, width = tokens.shape
    count = own_count // own_seqs
    head = query_gain.shape[0]
    heads_all = width // head
    heads = heads_all // 4
    cls = 2 * side + core
    own_items = own_seqs * items_seq
    dp_items = condition.shape[0]
    ringed = nmod == 2 and attend_out.shape[0] == head
    hid = feed_out.shape[0] // 2

    def swap_core(value):
        return lax.ppermute(value, "dp", [(i, i ^ 1) for i in range(ndp)])

    def swap_side(value):
        return lax.ppermute(value, "mod", [(i, i ^ 1) for i in range(nmod)])

    def pick(which, pair0, pair1):
        return jnp.where(which == 0, pair0, pair1)

    def ordered(which, own, other):
        return pick(which, own, other), pick(which, other, own)

    half = planes // 2

    def plane_of(ring):
        ring = lax.rem(ring + 2 * planes, planes)
        return jnp.where(ring < half, 2 * ring, 2 * (planes - 1 - ring) + 1)

    place = jnp.where(plane % 2 == 0, plane // 2, planes - 1 - plane // 2)

    def static_plane(ring):
        ring %= planes
        return 2 * ring if ring < half else 2 * (planes - 1 - ring) + 1

    def hop(value, step):
        pairs = [
            (2 * static_plane(r) + c, 2 * static_plane(r + step) + c)
            for r in range(planes)
            for c in range(2)
        ]
        return lax.ppermute(value, "dp", pairs)

    def ring_gather(block, slot=lambda index: index):
        out = jnp.zeros((planes,) + block.shape, block.dtype)
        cut = block.shape[0] // 32 * 16

        def put(out, piece, ring, row=0):
            start = (slot(plane_of(ring)), row) + (0,) * (block.ndim - 1)
            return lax.dynamic_update_slice(out, piece[None], start[: block.ndim + 1])

        out = put(out, block, place)
        ahead = behind = block
        for step in range(1, half):
            ahead, behind = hop(ahead, 1), hop(behind, -1)
            out = put(out, ahead, place - step)
            out = put(out, behind, place + step)
        ahead, behind = hop(ahead[:cut], 1), hop(behind[cut:], -1)
        out = put(out, ahead, place - half)
        return put(out, behind, place + half, cut)

    def ring_scatter(blocks, slot=lambda index: index):
        rows = blocks.shape[1]
        cut = rows // 32 * 16

        def take(ring, row, size):
            start = (slot(plane_of(ring)), row) + (0,) * (blocks.ndim - 2)
            return lax.dynamic_slice(blocks, start, (1, size) + blocks.shape[2:])[0]

        def plus(left, right):
            return (left.astype(F32) + right.astype(F32)).astype(BF)

        ahead = hop(take(place + half, 0, cut), 1)
        behind = hop(take(place - half, cut, rows - cut), -1)
        for step in range(half - 1, 0, -1):
            mine_ahead, mine_behind = take(place + step, 0, rows), take(place - step, 0, rows)
            if step == half - 1:
                ahead = jnp.concatenate([plus(mine_ahead[:cut], ahead), mine_ahead[cut:]], 0)
                behind = jnp.concatenate([mine_behind[:cut], plus(mine_behind[cut:], behind)], 0)
            else:
                ahead, behind = plus(mine_ahead, ahead), plus(mine_behind, behind)
            ahead, behind = hop(ahead, 1), hop(behind, -1)
        return take(place, 0, rows).astype(F32) + ahead.astype(F32) + behind.astype(F32)

    def spread_columns(parts):
        keep = pick(side, parts[0], parts[1])
        came = swap_side(pick(side, parts[1], parts[0]))
        both = jnp.concatenate(ordered(side, keep, came), axis=-1)
        keep = pick(core, both[0], both[1])
        came = swap_core(pick(core, both[1], both[0]))
        return jnp.concatenate(ordered(core, keep, came), axis=0)

    def unspread_columns(summed):
        rows, k = summed.shape[0] // 2, summed.shape[1] // 2
        top, low = summed[:rows], summed[rows:]
        came = swap_core(pick(core, low, top))
        both = jnp.stack(ordered(core, pick(core, top, low), came))
        left, right = both[:, :, :k], both[:, :, k:]
        came = swap_side(pick(side, right, left))
        return jnp.stack(ordered(side, pick(side, left, right), came))

    def gather_whole(weight):
        return lax.all_gather(
            lax.all_gather(weight, "mod", axis=1, tiled=True), "dp", axis=0, tiled=True
        )

    def scatter_whole(padded):
        padded = lax.psum_scatter(padded.astype(BF), "mod", scatter_dimension=1, tiled=True)
        return lax.psum_scatter(padded, "dp", scatter_dimension=0, tiled=True).astype(F32)

    def stack_other_core(value):
        return jnp.stack(ordered(core, value, swap_core(value)))

    def group(value):
        first = jnp.stack([value, swap_side(value)])
        return jnp.concatenate([first, swap_core(first)])

    whole_count = lengths.size + positions.size
    small = jnp.concatenate([lengths.reshape(-1), positions.reshape(-1)])
    small = group(small)
    lengths_g = small[:, : lengths.size].reshape(4 * own_seqs, items_seq)
    places_g = small[:, lengths.size : whole_count].reshape(4, 2, own_seqs, count)
    places_g = jnp.swapaxes(places_g, 1, 2).reshape(4 * own_seqs, 2, count)
    seqs = 4 * own_seqs

    cond_float = condition.astype(F32)
    silu_cond = jax.nn.silu(cond_float).astype(BF)
    silu_rows = lax.all_to_all(silu_cond, "dp", split_axis=1, concat_axis=0, tiled=True)
    partial = dot(silu_rows, modulate_weight)
    mod_cols = partial.shape[1]
    if ringed:
        partial = partial.reshape(planes, 2 * dp_items, 2, mod_cols // 2)
        left, right = partial[:, :, 0], partial[:, :, 1]
        came = swap_core(pick(core, right, left).astype(BF))
        kept = (pick(core, left, right) + came.astype(F32)).astype(BF)
        mods = ring_scatter(kept).astype(BF)
        mods = jnp.concatenate(ordered(core, mods, swap_core(mods)), axis=1)
        mods = jnp.concatenate(ordered(side, mods, swap_side(mods)), axis=1)
    else:
        mods = lax.psum_scatter(partial, "dp", scatter_dimension=0, tiled=True).astype(BF)
        mods = lax.all_gather(mods, "mod", axis=1, tiled=True)
        mods = stack_other_core(mods).reshape(2 * dp_items, 6 * width)

    columns_in = attend_in.shape[1]
    if ringed:
        parts = attend_in.reshape(head, columns_in // (4 * head), 4, head)
        parts = jnp.transpose(parts, (2, 0, 1, 3)).reshape(2, 2, head, columns_in // 4)
        w_in = ring_gather(spread_columns(parts)).reshape(width, 3 * heads * head)
        w_out = ring_gather(attend_out, lambda index: (index % 2) * half + index // 2)
        rows = feed_in.shape[0]
        parts = feed_in.reshape(rows, planes, 2, 2, hid)
        parts = jnp.transpose(parts, (3, 2, 0, 1, 4)).reshape(2, 2, rows, planes * hid)
        w_up = ring_gather(spread_columns(parts)).reshape(width, 2 * planes * hid)
        keep = pick(side, feed_out[:hid], feed_out[hid:])
        came = swap_side(pick(side, feed_out[hid:], feed_out[:hid]))
        w_down = jnp.concatenate(ordered(side, keep, came), axis=1)
        w_down = ring_gather(w_down).reshape(planes * hid, width)
        w_out = w_out.reshape(2, half * head, width // 2)
        w_out = jnp.concatenate(ordered(side, w_out, swap_side(w_out)), axis=2)
        w_out = jnp.stack(ordered(core, w_out, swap_core(w_out)), axis=1)
        w_out = w_out.reshape(4, heads * head, width)
    else:
        w_in = gather_whole(attend_in).reshape(width, 3 * heads, 4, head)
        w_in = lax.dynamic_index_in_dim(w_in, cls, 2, False).reshape(width, 3 * heads * head)
        w_out = gather_whole(attend_out).reshape(heads, 4, head, width)
        w_out = jnp.swapaxes(w_out, 0, 1).reshape(4, heads * head, width)
        share = 2 * core + side
        w_up = gather_whole(feed_in).reshape(width, 2 * planes, 4, hid)
        w_up = lax.dynamic_index_in_dim(w_up, share, 2, False).reshape(width, 2 * planes * hid)
        w_down = gather_whole(feed_out).reshape(planes, 4, hid, width)
        w_down = lax.dynamic_index_in_dim(w_down, share, 1, False).reshape(planes * hid, width)
    hidden_units = planes * hid

    inputs = group(tokens).reshape(4 * own_count, width).astype(F32)
    upstream = group(cotangent).reshape(4 * own_count, width).astype(F32)

    ends = jnp.cumsum(lengths_g, axis=1, dtype=jnp.int32)
    spots = jnp.arange(count, dtype=jnp.int32)
    items = jnp.sum(
        (spots[None, :, None] >= ends[:, None, :]).astype(jnp.int32), axis=2, dtype=jnp.int32
    )
    rel = jnp.arange(4, dtype=jnp.int32)
    base = (core ^ (rel // 2)) * dp_items + (mod ^ (rel % 2)) * own_items
    base = base[:, None] + jnp.arange(own_seqs, dtype=jnp.int32)[None, :] * items_seq
    index = (base.reshape(seqs, 1) + items).reshape(-1)
    members = index[:, None] == jnp.arange(2 * dp_items, dtype=jnp.int32)[None, :]
    members = members.astype(BF)
    own_index = jnp.arange(own_seqs, dtype=jnp.int32)[:, None] * items_seq + items[:own_seqs]
    own_members = own_index.reshape(-1)[:, None] == jnp.arange(own_items, dtype=jnp.int32)[None, :]
    own_members = own_members.astype(F32)

    def token_mod(block):
        return dot(members, mods[:, block * width : (block + 1) * width])

    shift_attend, scale_attend, gate_attend, shift_feed, scale_feed, gate_feed = (
        token_mod(block) for block in range(6)
    )

    quarter = head // 4
    entry = jnp.arange(head, dtype=jnp.int32)
    freq = jnp.power(10000.0, -(entry % quarter).astype(F32) / quarter)
    spot = jnp.where(
        (entry // (head // 2))[None, :, None] == 0, places_g[:, 0:1, :], places_g[:, 1:2, :]
    ).astype(F32)
    angle = spot * freq[None, :, None]
    cosine = jnp.cos(angle)
    sine = jnp.sin(angle)
    sine = jnp.where((entry % (head // 2) < quarter)[None, :, None], -sine, sine)
    qg = jnp.broadcast_to(query_gain[:, None], (head, count))
    kg = jnp.broadcast_to(key_gain[:, None], (head, count))
    item_row, item_col = items[:, None, :], items[:, :, None]

    normed_one, inverse_one = layer_norm(inputs)
    modded_one = (normed_one * (1.0 + scale_attend) + shift_attend).astype(BF)
    raw, low, mixed = attend_forward(
        modded_one, w_in, cosine, sine, qg, kg, item_row, item_col, heads
    )
    mixed_all = jnp.zeros((4,) + mixed.shape, BF)
    pair = jnp.stack([mixed, swap_side(mixed)])
    both = jnp.concatenate([pair, swap_core(pair)])
    both = both.reshape(4, heads * head, 4, own_count)
    for other in range(4):
        block = both[other]
        if other & 1:
            block = block.reshape(-1, 2, 2, own_count)[:, :, ::-1]
        if other & 2:
            block = block.reshape(-1, 2, 2, own_count)[:, ::-1]
        mixed_all = lax.dynamic_update_slice(
            mixed_all, block.reshape((1,) + mixed.shape), ((2 * (side ^ (other & 1))) + (core ^ (other >> 1)), 0, 0)
        )
    attended = dot(mixed_all.reshape(width, -1), w_out.reshape(width, width), 0, 0)
    resid = inputs + gate_attend * attended
    normed_two, inverse_two = layer_norm(resid)
    modded_two = (normed_two * (1.0 + scale_feed) + shift_feed).astype(BF)
    gate_up = dot(modded_two, w_up)
    gate_part, up_part = gate_up[:, :hidden_units], gate_up[:, hidden_units:]
    sigma = jax.nn.sigmoid(gate_part)
    silu_gate = gate_part * sigma
    hidden = (silu_gate * up_part).astype(BF)
    fed_part = dot(hidden, w_down).astype(BF)

    def group_sum(part):
        part = part.reshape(2, 2, own_count, width)
        part = (part[0].astype(F32) + swap_core(part[1]).astype(F32)).astype(BF)
        return part[0].astype(F32) + swap_side(part[1]).astype(F32)

    own_resid, own_upstream = resid[:own_count], upstream[:own_count]
    fed = group_sum(fed_part)
    block_out = (own_resid + gate_feed[:own_count] * fed).astype(BF)

    fed_grad = (gate_feed * upstream).astype(BF)
    hidden_grad = dot(fed_grad, w_down, 1, 1)
    slope = sigma * (1.0 + gate_part * (1.0 - sigma))
    gate_up_grad = jnp.concatenate(
        [hidden_grad * up_part * slope, hidden_grad * silu_gate], axis=1
    ).astype(BF)
    down_grad = dot(hidden, fed_grad, 0, 0).astype(BF)
    up_grad = dot(modded_two, gate_up_grad, 0, 0).astype(BF)
    m2 = group_sum(dot(gate_up_grad, w_up, 1, 1).astype(BF))
    own_normed_two = normed_two[:own_count]
    resid_grad = own_upstream + norm_back(
        m2 * (1.0 + scale_feed[:own_count]), own_normed_two, inverse_two[:own_count]
    )
    attended_grad = (gate_attend[:own_count] * resid_grad).astype(BF)
    attended_grad = group(attended_grad).reshape(4 * own_count, width)

    own_w_out = lax.dynamic_index_in_dim(w_out, cls, 0, False)
    projected_grad, query_gain_part, key_gain_part = attend_backward(
        attended_grad, own_w_out, raw, low, cosine, sine, qg, kg, item_row, item_col, heads
    )
    gains = jnp.stack([jnp.sum(query_gain_part, axis=1), jnp.sum(key_gain_part, axis=1)])
    core_mixed = mixed_all.reshape(2, 2, heads * head, -1)
    core_mixed = pick(core, core_mixed[:, 0], core_mixed[:, 1]).reshape(2 * heads * head, -1)
    side_grad = pick(side, attended_grad[:, : width // 2], attended_grad[:, width // 2 :])
    out_grad = dot(core_mixed, side_grad).astype(BF)
    in_grad = dot(modded_one, projected_grad, 0, 0).astype(BF)
    m1 = group_sum(dot(projected_grad, w_in, 1, 1).astype(BF))
    own_normed_one = normed_one[:own_count]
    tokens_grad = resid_grad + norm_back(
        m1 * (1.0 + scale_attend[:own_count]), own_normed_one, inverse_one[:own_count]
    )

    if ringed:
        down_sum = ring_scatter(down_grad.reshape(planes, hid, width)).astype(BF)
        left, right = down_sum[:, : width // 2], down_sum[:, width // 2 :]
        came = swap_side(pick(side, right, left))
        feed_out_grad = jnp.concatenate(
            ordered(side, pick(side, left, right), came), axis=0
        ).astype(F32)
        up_sum = ring_scatter(up_grad.reshape(planes, 2 * feed_in.shape[0], -1)).astype(BF)
        parts = unspread_columns(up_sum).reshape(2, 2, feed_in.shape[0], planes, hid)
        feed_in_grad = jnp.transpose(parts, (2, 3, 1, 0, 4)).reshape(feed_in.shape).astype(F32)
        attend_out_grad = ring_scatter(
            out_grad.reshape(planes, head, width // 2),
            lambda index: (index % 2) * half + index // 2,
        )
        in_sum = ring_scatter(in_grad.reshape(planes, 2 * head, -1)).astype(BF)
        parts = unspread_columns(in_sum).reshape(4, head, columns_in // (4 * head), head)
        attend_in_grad = jnp.transpose(parts, (1, 2, 0, 3)).reshape(attend_in.shape).astype(F32)
    else:

        def padded(shape, value, axis, which):
            zero = jnp.zeros(shape, value.dtype)
            return lax.dynamic_update_index_in_dim(zero, value, which, axis)

        grad = down_grad.reshape(planes, hid, width)
        grad = padded((planes, 4, hid, width), grad, 1, share)
        feed_out_grad = scatter_whole(grad.reshape(4 * hidden_units, width))
        grad = up_grad.reshape(width, 2 * planes, hid)
        grad = padded((width, 2 * planes, 4, hid), grad, 2, share)
        feed_in_grad = scatter_whole(grad.reshape(width, 8 * hidden_units))
        grad = out_grad.reshape(2, heads, head, width // 2)
        grad = jnp.swapaxes(grad, 0, 1)
        grad = padded((heads, 2, head, 2, width // 2), grad, 3, side)
        grad = padded((heads, 2, 2, head, 2, width // 2), grad, 2, core)
        attend_out_grad = scatter_whole(grad.reshape(width, width))
        grad = in_grad.reshape(width, 3 * heads, head)
        grad = padded((width, 3 * heads, 4, head), grad, 2, cls)
        attend_in_grad = scatter_whole(grad.reshape(width, 3 * width))

    terms = (
        m1,
        m1 * own_normed_one,
        resid_grad * attended[:own_count],
        m2,
        m2 * own_normed_two,
        own_upstream * fed,
    )
    mod_grad = jnp.concatenate(
        [
            lax.dot_general(own_members, term, (((0,), (0,)), ((), ())), precision=HIGHEST)
            for term in terms
        ],
        axis=1,
    ).astype(BF)
    if ringed:
        left, right = mod_grad[:, :mod_cols], mod_grad[:, mod_cols:]
        came = swap_side(pick(side, right, left))
        mod_grad = jnp.concatenate(ordered(side, pick(side, left, right), came), axis=0)
        mod_grad = ring_gather(mod_grad)
        mod_grad = jnp.stack(ordered(core, mod_grad, swap_core(mod_grad)), axis=1)
        mod_grad = mod_grad.reshape(ndp * dp_items, mod_cols)
    else:
        mod_grad = lax.all_to_all(mod_grad, "mod", split_axis=1, concat_axis=0, tiled=True)
        mod_grad = lax.all_gather(mod_grad, "dp", axis=0, tiled=True)
    modulate_grad = dot(silu_rows, mod_grad, 0, 0)
    cond_terms = dot(mod_grad, modulate_weight, 1, 1).astype(BF)
    cond_terms = lax.all_to_all(cond_terms, "dp", split_axis=0, concat_axis=1, tiled=True)
    own_width = width // nmod
    if ringed:
        left, right = cond_terms[:, :own_width], cond_terms[:, own_width:]
        came = swap_side(pick(side, right, left))
        cond_share = pick(side, left, right).astype(F32) + came.astype(F32)
    else:
        cond_share = lax.psum_scatter(
            cond_terms, "mod", scatter_dimension=1, tiled=True
        ).astype(F32)
    cond_cols = lax.dynamic_slice_in_dim(cond_float, mod * own_width, own_width, 1)
    cond_sigma = jax.nn.sigmoid(cond_cols)
    condition_grad = cond_share * cond_sigma * (1.0 + cond_cols * (1.0 - cond_sigma))
    gains = lax.psum(gains, ("dp", "mod"))
    return (
        block_out,
        tokens_grad,
        condition_grad,
        gains[0],
        gains[1],
        attend_in_grad,
        attend_out_grad,
        feed_in_grad,
        feed_out_grad,
        modulate_grad,
    )


def solution(mesh):
    rows = P(("dp", "mod"), None)
    both = P("dp", "mod")
    return jax.shard_map(
        body,
        mesh=mesh,
        in_specs=(
            rows,
            P("dp", None),
            rows,
            P(None, ("dp", "mod")),
            P(),
            P(),
            both,
            both,
            both,
            both,
            both,
            rows,
        ),
        out_specs=(rows, rows, both, P(), P(), both, both, both, both, both),
        check_vma=False,
    )
```

time: 971 us -> 712 us (0.73)
  waiting for transfers between devices: 518 us -> 200 us
  blocking collectives: 160 us -> 39.3 us
  local copies, waits for them, and re-layouts: 32.5 us -> 149 us
  matrix products: 162 us -> 81.2 us
  starting transfers between devices: 33.3 us -> 113 us
  other arithmetic: 38.8 us -> 86 us
  Pallas kernels: 0 us -> 28 us
  between operations: 16.2 us -> 3.07 us
    all_gather x7 -> x0, waiting for transfers between devices: 277 us -> none  [the longest x1 93.5 us: body(): lax.all_gather(lax.all_gather(feed_in, 'mod', axis=1, tiled=True), 'dp',...]
    ppermute x0 -> x113, waiting for transfers between devices: none -> 196 us  [the longest x79 149 us: hop(): return lax.ppermute(value, 'dp', pairs)]
    all_gather x10 -> x0, blocking collectives: 109 us -> none  [the longest x2 26.2 us: body(): lax.all_gather(kept[2], 'mod', axis=0, tiled=True)]
    reduce_scatter x3 -> x0, waiting for transfers between devices: 108 us -> none  [the longest x1 91.7 us: body(): lax.psum_scatter(weight_sums[2].astype(jnp.bfloat16), 'dp', scatter_dimen...]
    unnamed x16 -> x0, waiting for transfers between devices: 103 us -> none
    ppermute x0 -> x113, starting transfers between devices: none -> 103 us  [the longest x79 80.6 us: hop(): return lax.ppermute(value, 'dp', pairs)]
    dot_general x43 -> x25, matrix products: 162 us -> 81.2 us  [the longest x19 73.6 us: dot(): lax.dot_general(left, right, (((left_dim,), (right_dim,)), ((), ())), pre...]
    dynamic_update_slice x0 -> x45, local copies, waits for them, and re-layouts: none -> 38.8 us  [the longest x41 32.9 us: put(): return lax.dynamic_update_slice(out, piece[None], start[:block.ndim + 1])]
  transfers between devices with their start and end apart: 22 -> 115, of which waited for: 13 -> 49; matrix products, arithmetic and copies ran while one was open for 14% -> 29% of each run, Pallas kernels for 0% -> 1%
where the time goes in v1:
time: 712 us; the launch traced here: 699 us
  waiting for transfers between devices  200 us (28%)
  local copies, waits for them, and re-layouts  149 us (21%)
  starting transfers between devices  113 us (16%)
  other arithmetic  86 us (12%)
  matrix products  81.2 us (11%)
  blocking collectives  39.3 us (6%)
  Pallas kernels  28 us (4%)
    ppermute x79, waiting for transfers between devices, hop(): return lax.ppermute(value, 'dp', pairs)  149 us
    ppermute x79, starting transfers between devices, hop(): return lax.ppermute(value, 'dp', pairs)  80.6 us
    dot_general x19, matrix products, dot(): lax.dot_general(left, right, (((left_dim,), (right_dim,)), ((), ())), pre...  73.6 us
    ppermute x18, waiting for transfers between devices, swap_side(): return lax.ppermute(value, 'mod', [(i, i ^ 1) for i in range(nmod)])  46.4 us
    psum x1, blocking collectives, body(): gains = lax.psum(gains, ('dp', 'mod'))  39.3 us
    dynamic_update_slice x41, local copies, waits for them, and re-layouts, put(): return lax.dynamic_update_slice(out, piece[None], start[:block.ndim + 1])  32.9 us
    ppermute x18, starting transfers between devices, swap_side(): return lax.ppermute(value, 'mod', [(i, i ^ 1) for i in range(nmod)])  20.9 us
    pallas_call x1, Pallas kernels, attend_backward(): pl.pallas_call(functools.partial(attend_backward_kernel, heads, head), gr...  17.5 us
  transfers between devices with their start and end apart: 115, of which 49 were waited for; matrix products, arithmetic and copies ran while one was open for 29% of the time, Pallas kernels for 1%

profile of v1, /device:TPU:0, one launch (start us, length us, event | category | flops | bytes accessed | tf_op | source)
XLA Modules:
  0.0 699.2 jit_solution(16575051619062353201)
XLA Ops:
  8.8 5.9 all-to-all-start
  103.7 11.3 %collective-permute-done.19 = bf16[144,864]{0,1:T(8,128)(2,1)S(1)} collective-permute-done((bf16[144,864]{0,1:T(8,128)(2,1)}, bf16[144,864]{0,1:T(8,128)(2,1)S(1)}, u32[]{:S(2)}, u32[]{:S(2)}) %collective-permute-start.19) | collective-permute-done | bytes 248864 | tf_op jit(solution)/shard_map/ppermute | solution.py:291
  181.2 6.5 collective-permute-done.11
  236.3 10.5 %attend_forward.1 = (f32[8,576,128]{2,1,0:T(8,128)}, bf16[8,288,128]{2,1,0:T(8,128)(2,1)S(1)}, bf16[288,1024]{1,0:T(8,128)(2,1)S(1)}) custom-call(bf16[1024,1152]{1,0:T(8,128)(2,1)} %add_convert_fusion.1.modded_ref, bf16[1152,864]{1,0:T(8,128)(2,1)S(1)} %bitcast.483, f32[8,72,128]{2,1,0:T(8,128)S(1)} %get-tuple-element.121.cos_ref, ...), custom_call_target="tpu_custom_call" | custom-call | flops 2189426688 | bytes 10485760 | tf_op jit(solution)/shard_map/attend_forward/pallas_call | solution.py:161
  249.6 11.2 %collective-permute-done.25 = bf16[288,1024]{1,0:T(8,128)(2,1)S(1)} collective-permute-done((bf16[288,1024]{1,0:T(8,128)(2,1)S(1)}, bf16[288,1024]{1,0:T(8,128)(2,1)S(1)}, u32[]{:S(2)}, u32[]{:S(2)}) %collective-permute-start.25) | collective-permute-done | bytes 589856 | tf_op jit(solution)/shard_map/ppermute | solution.py:265
  267.6 7.6 %rev.10 = bf16[288,2,2,256]{3,2,1,0:T(2,128)(2,1)} reverse(bf16[288,2,2,256]{3,2,1,0:T(2,128)(2,1)} %reshape_squeeze.10), dimensions={2} | reverse | bytes 1179648 | tf_op jit(solution)/shard_map/rev | solution.py:474
  285.1 7.6 %rev.12 = bf16[288,2,2,256]{3,2,1,0:T(2,128)(2,1)} reverse(bf16[288,2,2,256]{3,2,1,0:T(2,128)(2,1)} %reshape_squeeze.12), dimensions={1,2} | reverse | bytes 1179648 | tf_op jit(solution)/shard_map/rev | solution.py:476
  307.3 6.1 fusion.118
  321.3 9.0 %fusion.119 = f32[1024,1536]{1,0:T(8,128)} fusion(bf16[1024,1152]{1,0:T(8,128)(2,1)S(1)} %add_convert_fusion, bf16[1152,1536]{1,0:T(8,128)(2,1)} %bitcast.76), kind=kOutput, calls=%fused_computation.431 | convolution fusion | flops 3623878656 | bytes 12189696 | tf_op jit(solution)/shard_map/dot_general | solution.py:31
  330.3 7.1 %multiply_convert_fusion.1 = (bf16[1024,768]{1,0:T(8,128)(2,1)}, bf16[1024,768]{1,0:T(8,128)(2,1)}, bf16[1024,768]{1,0:T(8,128)(2,1)}) fusion(f32[1024,1536]{1,0:T(8,128)} %fusion.119, bf16[1024,1152]{1,0:T(8,128)(2,1)S(1)} %copy-done.33, bf16[768,1152]{1,0:T(8,128)(2,1)S(1)} %bitcast.528), kind=kOutput, calls=%fused_computation.21 | convolution fusion | flops 1823735808 | bytes 15138816 | tf_op jit(solution)/shard_map/dot_general | solution.py:31
  337.4 8.6 %convolution_convert_fusion.2 = bf16[1024,1152]{1,0:T(8,128)(2,1)} fusion(bf16[1152,1536]{1,0:T(8,128)(2,1)} %bitcast.76, bf16[1024,768]{1,0:T(8,128)(2,1)} %get-tuple-element.33, bf16[1024,768]{1,0:T(8,128)(2,1)} %get-tuple-element.32), kind=kOutput, calls=%fused_computation.15 | convolution fusion | flops 3631349760 | bytes 9043968 | tf_op jit(solution)/shard_map/dot_general | solution.py:31
  346.0 6.5 convolution_convert_fusion
  374.3 5.9 collective-permute-done.105
  383.0 13.5 %collective-permute-done.106 = bf16[96,1152]{1,0:T(8,128)(2,1)S(1)} collective-permute-done((bf16[96,1152]{1,0:T(8,128)(2,1)S(1)}, bf16[96,1152]{1,0:T(8,128)(2,1)S(1)}, u32[]{:S(2)}, u32[]{:S(2)}) %collective-permute-start.106) | collective-permute-done | bytes 221216 | tf_op jit(solution)/shard_map/ppermute | solution.py:291
  397.6 7.4 %collective-permute-done.110 = bf16[96,1152]{1,0:T(8,128)(2,1)S(1)} collective-permute-done((bf16[96,1152]{1,0:T(8,128)(2,1)S(1)}, bf16[96,1152]{1,0:T(8,128)(2,1)S(1)}, u32[]{:S(2)}, u32[]{:S(2)}) %collective-permute-start.110) | collective-permute-done | bytes 221216 | tf_op jit(solution)/shard_map/ppermute | solution.py:291
  407.3 6.0 collective-permute-done.107
  418.0 7.0 %collective-permute-done.96 = bf16[144,1536]{1,0:T(8,128)(2,1)S(1)} collective-permute-done((bf16[144,1536]{1,0:T(8,128)(2,1)S(1)}, bf16[144,1536]{1,0:T(8,128)(2,1)S(1)}, u32[]{:S(2)}, u32[]{:S(2)}) %collective-permute-start.96) | collective-permute-done | bytes 442400 | tf_op jit(solution)/shard_map/ppermute | solution.py:291
  431.1 6.3 collective-permute-done.100
  438.9 6.1 collective-permute-done.61
  489.1 17.5 %attend_backward.1 = (bf16[1024,864]{1,0:T(8,128)(2,1)S(1)}, f32[72,128]{1,0:T(8,128)S(1)}, f32[72,128]{1,0:T(8,128)S(1)}) custom-call(bf16[1024,1152]{1,0:T(8,128)(2,1)} %bitcast.494, bf16[288,1152]{1,0:T(8,128)(2,1)S(1)} %dynamic-slice_bitcast_fusion.weight_ref, f32[8,576,128]{2,1,0:T(8,128)} %get-tuple-element.17.raw_ref, ...), custom_call_target="tpu_custom_call" | custom-call | flops 1056964608 | bytes 10485760 | tf_op jit(solution)/shard_map/attend_backward/pallas_call | solution.py:197
  537.4 39.3 %psum.7 = f32[2,72]{1,0:T(2,128)S(1)} all-reduce(f32[2,72]{1,0:T(2,128)S(1)} %pad_maximum_fusion.34), channel_id=1, replica_groups=mesh['dp'=16,'mod'=2] {'dp','mod'}, use_global_device_ids=true, to_apply=%region_12.13 | all-reduce | flops 144 | bytes 1152 | tf_op jit(solution)/shard_map/psum | solution.py:610
  589.7 7.0 %collective-permute-done.77 = bf16[144,864]{0,1:T(8,128)(2,1)S(1)} collective-permute-done((bf16[144,864]{0,1:T(8,128)(2,1)S(1)}, bf16[144,864]{0,1:T(8,128)(2,1)S(1)}, u32[]{:S(2)}, u32[]{:S(2)}) %collective-permute-start.77) | collective-permute-done | bytes 248864 | tf_op jit(solution)/shard_map/ppermute | solution.py:291
  600.0 7.0 %collective-permute-done.78 = bf16[144,864]{0,1:T(8,128)(2,1)S(1)} collective-permute-done((bf16[144,864]{0,1:T(8,128)(2,1)S(1)}, bf16[144,864]{0,1:T(8,128)(2,1)S(1)}, u32[]{:S(2)}, u32[]{:S(2)}) %collective-permute-start.78) | collective-permute-done | bytes 248864 | tf_op jit(solution)/shard_map/ppermute | solution.py:291
  626.7 15.6 %collective-permute-done.85 = bf16[2,72,432]{1,2,0:T(8,128)(2,1)S(1)} collective-permute-done((bf16[2,72,432]{1,2,0:T(8,128)(2,1)S(1)}, bf16[2,72,432]{1,2,0:T(8,128)(2,1)S(1)}, u32[]{:S(2)}, u32[]{:S(2)}) %collective-permute-start.85) | collective-permute-done | bytes 124448 | tf_op jit(solution)/shard_map/ppermute | solution.py:265
  (676 shorter events, 459.6 us)
Async XLA Ops:
  0.7 35.3 %collective-permute-start.28 = (bf16[72,576]{1,0:T(8,128)(2,1)}, bf16[72,576]{1,0:T(8,128)(2,1)}, u32[]{:S(2)}, u32[]{:S(2)}) collective-permute-start(bf16[72,576]{1,0:T(8,128)(2,1)} %param.19), channel_id=1, source_target_pairs={{0,4},{2,6},{8,0},{10,2},{16,8},{18,10},{24,16},{26,18},{28,24},{3... | collective-permute-start | bytes 248840 | tf_op jit(solution)/shard_map/ppermute | solution.py:291
  3.7 29.3 %collective-permute-start.27 = (bf16[72,576]{1,0:T(8,128)(2,1)}, bf16[72,576]{1,0:T(8,128)(2,1)}, u32[]{:S(2)}, u32[]{:S(2)}) collective-permute-start(bf16[72,576]{1,0:T(8,128)(2,1)} %param.19), channel_id=1, source_target_pairs={{0,8},{2,10},{8,16},{10,18},{16,24},{18,26},{24,28},{26,30},{28,20... | collective-permute-start | bytes 248840 | tf_op jit(solution)/shard_map/ppermute | solution.py:291
  33.0 67.6 %collective-permute-start = (bf16[256,1152]{1,0:T(8,128)(2,1)}, bf16[256,1152]{1,0:T(8,128)(2,1)}, u32[]{:S(2)}, u32[]{:S(2)}) collective-permute-start(bf16[256,1152]{1,0:T(8,128)(2,1)} %param.12), channel_id=1, source_target_pairs={{0,1},{1,0},{2,3},{3,2},{4,5},{5,4},{6,7},{7,6},{8,9},{9,8},{10,11... | collective-permute-start | bytes 1769480 | tf_op jit(solution)/shard_map/ppermute | solution.py:265
  36.0 60.9 %collective-permute-start.58 = (bf16[256,1152]{1,0:T(8,128)(2,1)}, bf16[256,1152]{1,0:T(8,128)(2,1)}, u32[]{:S(2)}, u32[]{:S(2)}) collective-permute-start(bf16[256,1152]{1,0:T(8,128)(2,1)} %param.23), channel_id=1, source_target_pairs={{0,1},{1,0},{2,3},{3,2},{4,5},{5,4},{6,7},{7,6},{8,9},{9,8},{10,11... | collective-permute-start | bytes 1769480 | tf_op jit(solution)/shard_map/ppermute | solution.py:265
  43.3 98.4 %collective-permute-start.4 = (bf16[8,32,1728]{2,1,0:T(8,128)(2,1)}, bf16[8,32,1728]{2,1,0:T(8,128)(2,1)}, u32[]{:S(2)}, u32[]{:S(2)}) collective-permute-start(bf16[8,32,1728]{2,1,0:T(8,128)(2,1)} %fusion.23), channel_id=1, source_target_pairs={{0,2},{2,0},{4,6},{6,4},{8,10},{10,8},{12,14},{14,12},{16,18},{18,... | collective-permute-start | bytes 2654216 | tf_op jit(solution)/shard_map/ppermute | solution.py:262
  80.2 65.1 %collective-permute-start.35 = (bf16[2,288,576]{2,1,0:T(8,128)(2,1)}, bf16[2,288,576]{2,1,0:T(8,128)(2,1)}, u32[]{:S(2)}, u32[]{:S(2)}) collective-permute-start(bf16[2,288,576]{2,1,0:T(8,128)(2,1)} %bitcast.59), channel_id=1, source_target_pairs={{0,1},{1,0},{2,3},{3,2},{4,5},{5,4},{6,7},{7,6},{8,9},{9,8},{10,11... | collective-permute-start | bytes 1990664 | tf_op jit(solution)/shard_map/ppermute | solution.py:265
  95.5 33.7 %collective-permute-start.39 = (bf16[144,1536]{1,0:T(8,128)(2,1)}, bf16[144,1536]{1,0:T(8,128)(2,1)}, u32[]{:S(2)}, u32[]{:S(2)}) collective-permute-start(bf16[144,1536]{1,0:T(8,128)(2,1)} %pad_maximum_fusion.13), channel_id=1, source_target_pairs={{0,8},{2,10},{8,16},{10,18},{16,24},{18,26},{24,28},{26,30},{28,20... | collective-permute-start | bytes 1327112 | tf_op jit(solution)/shard_map/ppermute | solution.py:291
  125.0 87.3 %collective-permute-start.1 = (bf16[2,256,1152]{2,1,0:T(8,128)(2,1)}, bf16[2,256,1152]{2,1,0:T(8,128)(2,1)}, u32[]{:S(2)}, u32[]{:S(2)}) collective-permute-start(bf16[2,256,1152]{2,1,0:T(8,128)(2,1)} %pad_maximum_fusion.8), channel_id=1, source_target_pairs={{0,2},{2,0},{4,6},{6,4},{8,10},{10,8},{12,14},{14,12},{16,18},{18,... | collective-permute-start | bytes 3538952 | tf_op jit(solution)/shard_map/ppermute | solution.py:262
  139.5 82.5 %collective-permute-start.59 = (bf16[2,256,1152]{2,1,0:T(8,128)(2,1)}, bf16[2,256,1152]{2,1,0:T(8,128)(2,1)}, u32[]{:S(2)}, u32[]{:S(2)}) collective-permute-start(bf16[2,256,1152]{2,1,0:T(8,128)(2,1)} %pad_maximum_fusion.10), channel_id=1, source_target_pairs={{0,2},{2,0},{4,6},{6,4},{8,10},{10,8},{12,14},{14,12},{16,18},{18,... | collective-permute-start | bytes 3538952 | tf_op jit(solution)/shard_map/ppermute | solution.py:262
  192.5 69.5 %collective-permute-start.36 = (bf16[2,288,1152]{2,1,0:T(8,128)(2,1)S(1)}, bf16[2,288,1152]{2,1,0:T(8,128)(2,1)S(1)}, u32[]{:S(2)}, u32[]{:S(2)}) collective-permute-start(bf16[2,288,1152]{2,1,0:T(8,128)(2,1)S(1)} %copy-done.42), channel_id=1, source_target_pairs={{0,2},{2,0},{4,6},{6,4},{8,10},{10,8},{12,14},{14,12},{16,18},{18,... | collective-permute-start | bytes 3981320 | tf_op jit(solution)/shard_map/ppermute | solution.py:262
  211.3 36.9 %collective-permute-start.45 = (bf16[64,1536]{1,0:T(8,128)(2,1)S(1)}, bf16[64,1536]{1,0:T(8,128)(2,1)S(1)}, u32[]{:S(2)}, u32[]{:S(2)}) collective-permute-start(bf16[64,1536]{1,0:T(8,128)(2,1)S(1)} %slice.498), channel_id=1, source_target_pairs={{0,8},{2,10},{8,16},{10,18},{16,24},{18,26},{24,28},{26,30},{28,20... | collective-permute-start | bytes 589832 | tf_op jit(solution)/shard_map/ppermute | solution.py:291
  212.3 36.6 %collective-permute-start.46 = (bf16[80,1536]{1,0:T(8,128)(2,1)S(1)}, bf16[80,1536]{1,0:T(8,128)(2,1)S(1)}, u32[]{:S(2)}, u32[]{:S(2)}) collective-permute-start(bf16[80,1536]{1,0:T(8,128)(2,1)S(1)} %slice.499), channel_id=1, source_target_pairs={{0,4},{2,6},{8,0},{10,2},{16,8},{18,10},{24,16},{26,18},{28,24},{3... | collective-permute-start | bytes 737288 | tf_op jit(solution)/shard_map/ppermute | solution.py:291
  367.5 62.2 %collective-permute-start.56 = (bf16[2,256,1152]{2,1,0:T(8,128)(2,1)}, bf16[2,256,1152]{2,1,0:T(8,128)(2,1)S(1)}, u32[]{:S(2)}, u32[]{:S(2)}) collective-permute-start(bf16[2,256,1152]{2,1,0:T(8,128)(2,1)} %bitcast.88), channel_id=1, source_target_pairs={{0,2},{2,0},{4,6},{6,4},{8,10},{10,8},{12,14},{14,12},{16,18},{18,... | collective-permute-start | bytes 3538952 | tf_op jit(solution)/shard_map/ppermute | solution.py:262
  371.8 56.5 %collective-permute-start.60 = (bf16[2,256,1152]{2,1,0:T(8,128)(2,1)S(1)}, bf16[2,256,1152]{2,1,0:T(8,128)(2,1)S(1)}, u32[]{:S(2)}, u32[]{:S(2)}) collective-permute-start(bf16[2,256,1152]{2,1,0:T(8,128)(2,1)S(1)} %bitcast.533), channel_id=1, source_target_pairs={{0,2},{2,0},{4,6},{6,4},{8,10},{10,8},{12,14},{14,12},{16,18},{18,... | collective-permute-start | bytes 3538952 | tf_op jit(solution)/shard_map/ppermute | solution.py:262
  380.2 26.4 %collective-permute-start.95 = (bf16[144,1536]{1,0:T(8,128)(2,1)S(1)}, bf16[144,1536]{1,0:T(8,128)(2,1)S(1)}, u32[]{:S(2)}, u32[]{:S(2)}) collective-permute-start(bf16[144,1536]{1,0:T(8,128)(2,1)S(1)} %pad_maximum_fusion.17), channel_id=1, source_target_pairs={{0,8},{2,10},{8,16},{10,18},{16,24},{18,26},{24,28},{26,30},{28,20... | collective-permute-start | bytes 1327112 | tf_op jit(solution)/shard_map/ppermute | solution.py:291
  425.2 33.8 %collective-permute-start.97 = (bf16[144,1536]{1,0:T(8,128)(2,1)S(1)}, bf16[144,1536]{1,0:T(8,128)(2,1)}, u32[]{:S(2)}, u32[]{:S(2)}) collective-permute-start(bf16[144,1536]{1,0:T(8,128)(2,1)S(1)} %get-tuple-element.35), channel_id=1, source_target_pairs={{0,8},{2,10},{8,16},{10,18},{16,24},{18,26},{24,28},{26,30},{28,20... | collective-permute-start | bytes 1327112 | tf_op jit(solution)/shard_map/ppermute | solution.py:291
  430.1 24.0 %collective-permute-start.57 = (bf16[256,1152]{1,0:T(8,128)(2,1)S(1)}, bf16[256,1152]{1,0:T(8,128)(2,1)S(1)}, u32[]{:S(2)}, u32[]{:S(2)}) collective-permute-start(bf16[256,1152]{1,0:T(8,128)(2,1)S(1)} %slice_bitcast_fusion.6), channel_id=1, source_target_pairs={{0,1},{1,0},{2,3},{3,2},{4,5},{5,4},{6,7},{7,6},{8,9},{9,8},{10,11... | collective-permute-start | bytes 1769480 | tf_op jit(solution)/shard_map/ppermute | solution.py:265
  461.7 24.0 %collective-permute-start.63 = (bf16[2,256,1152]{2,1,0:T(8,128)(2,1)}, bf16[2,256,1152]{2,1,0:T(8,128)(2,1)}, u32[]{:S(2)}, u32[]{:S(2)}) collective-permute-start(bf16[2,256,1152]{2,1,0:T(8,128)(2,1)} %pad_maximum_fusion.11), channel_id=1, source_target_pairs={{0,2},{2,0},{4,6},{6,4},{8,10},{10,8},{12,14},{14,12},{16,18},{18,... | collective-permute-start | bytes 3538952 | tf_op jit(solution)/shard_map/ppermute | solution.py:262
  522.1 54.6 %collective-permute-start.86 = (bf16[32,576]{1,0:T(8,128)(2,1)}, bf16[32,576]{1,0:T(8,128)(2,1)}, u32[]{:S(2)}, u32[]{:S(2)}) collective-permute-start(bf16[32,576]{1,0:T(8,128)(2,1)} %get-tuple-element.84), channel_id=1, source_target_pairs={{0,8},{2,10},{8,16},{10,18},{16,24},{18,26},{24,28},{26,30},{28,20... | collective-permute-start | bytes 110600 | tf_op jit(solution)/shard_map/ppermute | solution.py:291
  524.3 53.9 %collective-permute-start.90 = (bf16[40,576]{1,0:T(8,128)(2,1)}, bf16[40,576]{1,0:T(8,128)(2,1)}, u32[]{:S(2)}, u32[]{:S(2)}) collective-permute-start(bf16[40,576]{1,0:T(8,128)(2,1)} %get-tuple-element.87), channel_id=1, source_target_pairs={{0,4},{2,6},{8,0},{10,2},{16,8},{18,10},{24,16},{26,18},{28,24},{3... | collective-permute-start | bytes 138248 | tf_op jit(solution)/shard_map/ppermute | solution.py:291
  529.5 52.7 %collective-permute-start.76 = (bf16[64,864]{0,1:T(8,128)(2,1)}, bf16[64,864]{0,1:T(8,128)(2,1)}, u32[]{:S(2)}, u32[]{:S(2)}) collective-permute-start(bf16[64,864]{0,1:T(8,128)(2,1)} %bitcast.551), channel_id=1, source_target_pairs={{0,8},{2,10},{8,16},{10,18},{16,24},{18,26},{24,28},{26,30},{28,20... | collective-permute-start | bytes 331784 | tf_op jit(solution)/shard_map/ppermute | solution.py:291
  532.7 54.7 %collective-permute-start.80 = (bf16[80,864]{0,1:T(8,128)(2,1)}, bf16[80,864]{0,1:T(8,128)(2,1)}, u32[]{:S(2)}, u32[]{:S(2)}) collective-permute-start(bf16[80,864]{0,1:T(8,128)(2,1)} %bitcast.550), channel_id=1, source_target_pairs={{0,4},{2,6},{8,0},{10,2},{16,8},{18,10},{24,16},{26,18},{28,24},{3... | collective-permute-start | bytes 414728 | tf_op jit(solution)/shard_map/ppermute | solution.py:291
  580.5 30.4 %collective-permute-start.91 = (bf16[72,576]{1,0:T(8,128)(2,1)}, bf16[72,576]{1,0:T(8,128)(2,1)}, u32[]{:S(2)}, u32[]{:S(2)}) collective-permute-start(bf16[72,576]{1,0:T(8,128)(2,1)} %pad_maximum_fusion.31), channel_id=1, source_target_pairs={{0,4},{2,6},{8,0},{10,2},{16,8},{18,10},{24,16},{26,18},{28,24},{3... | collective-permute-start | bytes 248840 | tf_op jit(solution)/shard_map/ppermute | solution.py:291
  586.4 24.6 %collective-permute-start.88 = (bf16[72,576]{1,0:T(8,128)(2,1)}, bf16[72,576]{1,0:T(8,128)(2,1)}, u32[]{:S(2)}, u32[]{:S(2)}) collective-permute-start(bf16[72,576]{1,0:T(8,128)(2,1)} %fusion.76), channel_id=1, source_target_pairs={{0,8},{2,10},{8,16},{10,18},{16,24},{18,26},{24,28},{26,30},{28,20... | collective-permute-start | bytes 248840 | tf_op jit(solution)/shard_map/ppermute | solution.py:291
  (174 other events, 1788.0 us)
